TPU v7x, 32 devices: a whole 2x2x4 slice. The times are simulated.
32 devices in a mesh: group: 2 (over y), blk: 16 (over z, x, core).
Axes of the slice: x: 2, y: 2, z: 4, core: 2. Of those that a mesh axis runs over, the one named last changes fastest.
Arguments:
- student_hidden: bfloat16 [64, 4096], P(('group', 'blk')), parts along dimension 0, may hold values from -512 to 512
- teacher_hidden: bfloat16 [64, 1, 5120], P(('group', 'blk')), parts along dimension 0, may hold values from -512 to 512
- counts: int32 [64], P(('group', 'blk')), parts along dimension 0, may hold values from 0 to 7
- student_head: bfloat16 [8192, 10240], P('group', 'blk'), parts along dimension 0, may hold values from -16 to 16
- teacher_head: bfloat16 [1, 10240, 10240], P(None, 'group', 'blk'), parts along dimension 1, may hold values from -16 to 16
Outputs:
- row_loss: float32 [64], P(('group', 'blk')), parts along dimension 0
- grad_hidden: bfloat16 [64, 4096], P(('group', 'blk')), parts along dimension 0
There are 2 independent parts, one for each index of `group`. A program takes and returns all parts, laid end to end along the dimension named above; each array names one. Nothing has to cross between parts.
All inputs are finite; a program needn't handle non-finite values.
Results may differ from a plain program's by a relative error of at most 0.0046.
Values may be sent and summed in bfloat16 or wider, within the bound.
A program may use at most 64 MiB of HBM per device.

v0:
```python
import jax
import jax.numpy as jnp
from jax import lax
from jax.sharding import PartitionSpec as P

TEACH = 1


def on_device(student_hidden, teacher_hidden, counts, student_head, teacher_head):
    row_dev = student_hidden.shape[0]
    all_rows = row_dev * lax.axis_size("blk")
    pieces = lax.all_gather((student_hidden, teacher_hidden), "blk", axis=0, tiled=True)
    student_part = jnp.dot(pieces[0], student_head, preferred_element_type=jnp.float32)
    teacher_part = jnp.einsum(
        "rtd,tdv->rv", pieces[1], teacher_head, preferred_element_type=jnp.float32
    )
    student_part, poe_part = (student_part, teacher_part / TEACH)
    both = jnp.stack([student_part, poe_part])
    student_logit = both[0]
    poe_score = both[1]
    local_count = jnp.sum(counts).astype(jnp.float32)
    peak_student, peak_poe = lax.pmax(
        (jnp.max(student_logit, axis=1), jnp.max(poe_score, axis=1)), "blk"
    )
    shifted_poe = jnp.exp(poe_score - peak_poe[:, None])
    sum_student, sum_poe, weighted, total_count = lax.psum(
        (
            jnp.sum(jnp.exp(student_logit - peak_student[:, None]), axis=1),
            jnp.sum(shifted_poe, axis=1),
            jnp.sum(shifted_poe * (poe_score - student_logit), axis=1),
            local_count,
        ),
        "blk",
    )
    lse_student = peak_student + jnp.log(sum_student)
    lse_poe = peak_poe + jnp.log(sum_poe)
    divergence = weighted / sum_poe - lse_poe + lse_student
    first_row = lax.axis_index("blk") * row_dev
    own_divergence = lax.dynamic_slice_in_dim(divergence, first_row, row_dev)
    omega = counts.astype(jnp.float32) * all_rows / total_count
    row_loss = omega * own_divergence
    coeff = (
        jnp.exp(student_logit - lse_student[:, None]) - jnp.exp(poe_score - lse_poe[:, None])
    ).astype(jnp.bfloat16)
    partial_value = lax.psum_scatter(
        lax.dot_general(
            coeff, student_head, (((1,), (1,)), ((), ())), preferred_element_type=jnp.float32
        ),
        "blk",
        scatter_dimension=0,
        tiled=True,
    )
    grad_hidden = (partial_value * omega[:, None]).astype(jnp.bfloat16)
    return (row_loss, grad_hidden)


def solution(mesh):
    return jax.shard_map(
        on_device,
        mesh=mesh,
        in_specs=(
            P(("group", "blk"), None),
            P(("group", "blk"), None, None),
            P(("group", "blk")),
            P("group", "blk"),
            P(None, "group", "blk"),
        ),
        out_specs=(P(("group", "blk")), P(("group", "blk"), None)),
        check_vma=False,
    )
```

profile of v0, /device:TPU:0, one launch (start us, length us, event | category | flops | bytes accessed | tf_op | source)
XLA Modules:
  0.0 221.0 jit_solution(6498946699096393245)
XLA Ops:
  7.2 0.0 all-reduce.5.cloned.1.call-start
  7.2 1.3 reduce_sum.36
  9.2 0.8 copy.8
  9.9 25.1 %all_gather.6 = bf16[32,1,5120]{2,1,0:T(2,128)(2,1)S(1)} all-gather(bf16[2,1,5120]{2,1,0:T(2,128)(2,1)S(1)} %copy.8), channel_id=1, replica_groups=mesh['group'=2,'blk'=16] {'blk'}, dimensions={0}, use_global_device_ids=true | all-gather | bytes 348160 | tf_op jit(solution)/shard_map/all_gather | solution.py:12
  35.0 18.4 %all-gather = bf16[16,2,4096]{2,1,0:T(2,128)(2,1)S(1)} all-gather(bf16[1,2,4096]{2,1,0:T(2,128)(2,1)} %bitcast.15), channel_id=1, replica_groups=mesh['group'=2,'blk'=16] {'blk'}, dimensions={0}, use_global_device_ids=true | all-gather | bytes 278528 | tf_op jit(solution)/shard_map/all_gather | solution.py:12
  53.4 0.1 reshape.18
  53.5 0.0 copy-start
  53.5 4.2 %fusion.9 = (f32[32]{0:T(128)S(1)}, f32[32,640]{1,0:T(8,128)S(1)}) fusion(bf16[1,5120,640]{2,1,0:T(8,128)(2,1)} %param.9, bf16[32,1,5120]{2,1,0:T(2,128)(2,1)S(1)} %all_gather.6), kind=kOutput, calls=%fused_computation.19 | convolution fusion | flops 209735648 | bytes 6963328 | tf_op jit(solution)/shard_map/rtd,tdv->rv/dot_general | solution.py:14
  57.7 0.1 copy-done
  57.8 0.0 copy-start.2
  57.8 0.0 copy-start.1
  57.9 1.0 fusion.10
  58.9 31.1 %all-reduce.2 = (f32[32]{0:T(128)S(1)}, f32[32]{0:T(128)S(1)}) all-reduce(f32[32]{0:T(128)S(1)} %get-tuple-element.16, f32[32]{0:T(128)S(1)} %get-tuple-element.18), channel_id=1, replica_groups=mesh['group'=2,'blk'=16] {'blk'}, use_global_device_ids=true, to_apply=%region_3.0 | all-reduce | flops 64 | bytes 512 | tf_op jit(solution)/shard_map/pmax | solution.py:22
  89.9 0.2 multiply_reduce_fusion
  90.2 30.0 %all-reduce.1 = (f32[]{:T(128)}, f32[32]{0:T(128)S(1)}, f32[32]{0:T(128)S(1)}, f32[32]{0:T(128)S(1)}) all-reduce(f32[]{:T(128)S(6)} %convert_element_type.13, f32[32]{0:T(128)S(1)} %get-tuple-element.4, f32[32]{0:T(128)S(1)} %get-tuple-element.3, f32[32]{0:T(128)S(1)} %get-tuple-element.2), channel_id=1, replica_groups=mesh['group'=2,'blk'=16] {'blk'}, use_global_device_ids=true, to_apply=%region_1.0 | all-reduce | flops 97 | bytes 776 | tf_op jit(solution)/shard_map/psum | solution.py:26
  120.2 5.0 %fusion.5 = f32[32,4096]{1,0:T(8,128)} fusion(bf16[4096,640]{1,0:T(8,128)(2,1)} %param.8, f32[32,640]{1,0:T(8,128)S(1)} %get-tuple-element.17, f32[32,640]{1,0:T(8,128)S(1)} %get-tuple-element.19, f32[32]{0:T(128)S(1)} %get-tuple-element.14, f32[32]{0:T(128)S(1)} %get-tuple-element.15), kind=kOutput, calls=%fused_computation.9 | convolution fusion | flops 167854080 | bytes 5931264 | tf_op jit(solution)/shard_map/dot_general | solution.py:46
  125.1 0.0 all-reduce.5.cloned.1.call-update
  125.2 0.0 copy-done.2
  125.2 0.6 dynamic-slice
  126.4 0.0 copy-done.1
  126.4 1.2 dynamic-slice_multiply_fusion.1
  127.7 84.9 %all-reduce.5.cloned.1.call-done = f32[32,4096]{1,0:T(8,128)} async-done(((f32[32,4096]{1,0:T(8,128)}), f32[32,4096]{1,0:T(8,128)}) %all-reduce.5.cloned.1.call-update) | async-done | bytes 524304
  212.5 1.6 fusion.8
  (1 shorter events, 0.0 us)
Async XLA Ops:
  7.2 205.4 %all-reduce.5.cloned.1.call-start = ((), (), s32[]{:S(2)}) async-start(), calls=%async_computation | async-start | bytes 1048576
  53.5 4.4 %copy-start = (bf16[4096,640]{1,0:T(8,128)(2,1)S(1)}, bf16[4096,640]{1,0:T(8,128)(2,1)}, u32[]{:S(2)}) copy-start(bf16[4096,640]{1,0:T(8,128)(2,1)} %param.8) | copy-start | bytes 15728644
  57.8 67.3 %copy-start.2 = (u32[32]{0:T(128)S(1)}, u32[32]{0:T(128)}, u32[]{:S(2)}) copy-start(u32[32]{0:T(128)} %constant.22) | copy-start | bytes 388
  57.8 68.6 %copy-start.1 = (s32[2]{0:T(128)S(1)}, s32[2]{0:T(128)}, u32[]{:S(2)}) copy-start(s32[2]{0:T(128)} %param.7) | copy-start | bytes 28
Sparse Core Ops, SparseCore 0:
  125.3 87.2 all-reduce.4
where the time goes:
time: 221 us
  blocking collectives  105 us (48%)
  waiting for transfers between devices  84.9 us (38%)
  between operations  15.4 us (7%)
  matrix products  10.2 us (5%)
  other arithmetic  4.36 us (2%)
    unnamed x2, waiting for transfers between devices  84.9 us
    all_gather x2, blocking collectives, on_device(): lax.all_gather((student_hidden, teacher_hidden), 'blk', axis=0, tiled=True)  43.5 us
    pmax x1, blocking collectives, on_device(): lax.pmax((jnp.max(student_logit, axis=1), jnp.max(poe_score, axis=1)), 'b...  31.1 us
    psum x1, blocking collectives, on_device(): lax.psum((jnp.sum(jnp.exp(student_logit - peak_student[:, None]), axis=1)...  30 us
    dot_general x1, matrix products, on_device(): lax.dot_general(coeff, student_head, (((1,), (1,)), ((), ())), preferred_...  4.98 us
  transfers between devices with their start and end apart: 1, of which 1 were waited for; matrix products, arithmetic and copies ran while one was open for 1% of the time, Pallas kernels for 0%

commit v1 on v0

v1 whole, which is shorter than its diff:
```python
import functools

import jax
import jax.numpy as jnp
from jax import lax
from jax.experimental import pallas as pl
from jax.experimental.pallas import tpu as pltpu
from jax.sharding import PartitionSpec as P

MESH = pl.DeviceIdType.MESH
F32 = jnp.float32
BF16 = jnp.bfloat16
CUTS = 2


def kernel(
    n, far, counts_ref, sh_ref, th_ref, sw_ref, tw_ref, loss_ref, grad_ref,
    sheld, theld, xs, xt, sw, tw, part, outbox, inbox, stats, table,
    w_sem, send_sem, recv_sem, stat_send, stat_recv, part_send, part_recv,
):
    row_dev, ds = sh_ref.shape
    dt = th_ref.shape[1]
    rows = n * row_dev
    near = n // (2 * far)
    me = lax.axis_index("blk")
    core = lax.rem(me, 2)
    b = lax.rem(me // 2, near)
    a = me // (2 * near)
    wide = ds // CUTS

    def index(da, db, dc):
        return (
            lax.rem(a + da + far, far) * near + lax.rem(b + db + near, near)
        ) * 2 + lax.rem(core + dc, 2)

    weights = []
    for which, (src, dst) in enumerate(((sw_ref, sw), (tw_ref, tw))):
        step = src.shape[0] // 4
        for k in range(4):
            copy = pltpu.make_async_copy(
                src.at[pl.ds(k * step, step)], dst.at[pl.ds(k * step, step)], w_sem.at[which, k]
            )
            copy.start()
            weights.append(copy)

    barrier = pltpu.get_barrier_semaphore()

    def greet(k, carry):
        pl.semaphore_signal(
            barrier, inc=1, device_id={"blk": lax.rem(me + k, n)}, device_id_type=MESH
        )
        return carry

    lax.fori_loop(1, n, greet, 0)
    pl.semaphore_wait(barrier, n - 1)

    sends = []
    used = [0, 0]

    def send(which, src, slot, target):
        held = (sheld, theld)[which]
        copy = pltpu.make_async_remote_copy(
            src_ref=src,
            dst_ref=held.at[slot],
            send_sem=send_sem.at[which, used[which]],
            recv_sem=recv_sem.at[which, slot],
            device_id={"blk": target},
            device_id_type=MESH,
        )
        used[which] += 1
        copy.start()
        sends.append(copy)

    def arrive(which, slot):
        held = (sheld, theld)[which]
        pltpu.make_async_remote_copy(
            src_ref=held.at[slot],
            dst_ref=held.at[slot],
            send_sem=send_sem.at[which, 0],
            recv_sem=recv_sem.at[which, slot],
            device_id={"blk": me},
            device_id_type=MESH,
        ).wait_recv()

    for which, own in enumerate((sh_ref, th_ref)):
        for da in range(1, far):
            send(which, own, me, index(da, 0, 0))
        for db in range(1, near):
            send(which, own, me, index(0, db, 0))
        send(which, own, me, index(0, 0, 1))
    for which, own in enumerate((sh_ref, th_ref)):
        for da in range(1, far):
            slot = index(-da, 0, 0)
            arrive(which, slot)
            held = (sheld, theld)[which].at[slot]
            for db in range(1, near):
                send(which, held, slot, index(0, db, 0))
            send(which, held, slot, index(0, 0, 1))
        for db in range(1, near):
            for da in range(far):
                slot = index(-da, -db, 0)
                arrive(which, slot)
                send(which, (sheld, theld)[which].at[slot], slot, index(0, 0, 1))

    def product(which, x, w, width):
        held = (sheld, theld)[which]
        own = (sh_ref, th_ref)[which]
        for db in range(near):
            for da in range(far):
                arrive(which, index(-da, -db, 1))
        held[me] = own[...]
        for d in range(n):
            x[pl.ds(d * row_dev, row_dev), :] = held[d].astype(F32)
        for copy in weights[4 * which:4 * which + 4]:
            copy.wait()
        cut = width // 8

        def body(k, total):
            at = pl.ds(pl.multiple_of(k * cut, cut), cut)
            return total + jnp.dot(
                x[:, at].astype(BF16), w[at, :], preferred_element_type=F32
            )

        return lax.fori_loop(0, 8, body, jnp.zeros((rows, w.shape[1]), F32))

    student = product(0, xs, sw, ds)
    score = product(1, xt, tw, dt)

    peak_s = jnp.max(student, axis=1, keepdims=True)
    peak_p = jnp.max(score, axis=1, keepdims=True)
    exp_p = jnp.exp(score - peak_p)
    sum_s = jnp.sum(jnp.exp(student - peak_s), axis=1, keepdims=True)
    sum_p = jnp.sum(exp_p, axis=1, keepdims=True)
    weighted = jnp.sum(exp_p * (score - student), axis=1, keepdims=True)
    own_count = counts_ref[0]
    for r in range(1, row_dev):
        own_count = own_count + counts_ref[r]
    padded = table.shape[0]
    lane = lax.broadcasted_iota(jnp.int32, (rows, 128), 1)
    packed = jnp.where(lane == 5, own_count.astype(F32), 0.0)
    for k, column in enumerate((peak_s, sum_s, peak_p, sum_p, weighted)):
        packed = jnp.where(lane == k, column, packed)
    table[pl.ds(0, rows), :] = packed
    if padded > rows:
        table[pl.ds(rows, padded - rows), :] = jnp.zeros((padded - rows, 128), F32)
    stats[me] = jnp.transpose(table[...])[:8, :]

    def stat_copy(k):
        return pltpu.make_async_remote_copy(
            src_ref=stats.at[me],
            dst_ref=stats.at[me],
            send_sem=stat_send.at[k],
            recv_sem=stat_recv.at[me],
            device_id={"blk": lax.rem(me + k, n)},
            device_id_type=MESH,
        )

    def stat_start(k, carry):
        stat_copy(k).start()
        return carry

    def stat_wait(k, carry):
        slot = lax.rem(me + k, n)
        pltpu.make_async_remote_copy(
            src_ref=stats.at[slot],
            dst_ref=stats.at[slot],
            send_sem=stat_send.at[k],
            recv_sem=stat_recv.at[slot],
            device_id={"blk": me},
            device_id_type=MESH,
        ).wait_recv()
        return carry

    lax.fori_loop(1, n, stat_start, 0)
    lax.fori_loop(1, n, stat_wait, 0)

    all_stats = stats[...]
    top_s = jnp.max(all_stats[:, 0:1, :], axis=0)
    top_p = jnp.max(all_stats[:, 2:3, :], axis=0)
    scale_p = jnp.exp(all_stats[:, 2:3, :] - top_p[None])
    total_s = jnp.sum(jnp.exp(all_stats[:, 0:1, :] - top_s[None]) * all_stats[:, 1:2, :], axis=0)
    total_p = jnp.sum(scale_p * all_stats[:, 3:4, :], axis=0)
    total_w = jnp.sum(scale_p * all_stats[:, 4:5, :], axis=0)
    total_count = jnp.sum(all_stats[:, 5:6, :], axis=0)
    lse_s = top_s + jnp.log(total_s)
    lse_p = top_p + jnp.log(total_p)
    divergence = total_w / total_p - lse_p + lse_s
    line = lax.broadcasted_iota(jnp.int32, (128, padded), 0)
    merged = jnp.where(line == 0, lse_s, 0.0)
    merged = jnp.where(line == 1, lse_p, merged)
    merged = jnp.where(line == 2, divergence, merged)
    merged = jnp.where(line == 3, total_count, merged)
    table[...] = jnp.transpose(merged)

    coeff = (
        jnp.exp(student - table[pl.ds(0, rows), 0:1]) - jnp.exp(score - table[pl.ds(0, rows), 1:2])
    ).astype(BF16)

    own_rows = table[pl.ds(me * row_dev, row_dev), :]
    row = lax.broadcasted_iota(jnp.int32, (row_dev, 1), 0)
    own_counts = jnp.zeros((row_dev, 1), F32)
    for r in range(row_dev):
        own_counts = jnp.where(row == r, counts_ref[r].astype(F32), own_counts)
    omega = own_counts * rows / own_rows[:, 3:4]
    loss_ref[...] = jnp.broadcast_to(omega * own_rows[:, 2:3], loss_ref.shape)

    def part_copy(h, k):
        target = lax.rem(me + k, n)
        return pltpu.make_async_remote_copy(
            src_ref=outbox.at[h, target],
            dst_ref=inbox.at[h, me],
            send_sem=part_send.at[h, k],
            recv_sem=part_recv.at[h, me],
            device_id={"blk": target},
            device_id_type=MESH,
        )

    strip = 512 if wide % 512 == 0 else wide
    for h in range(CUTS):

        def grad_body(k, carry, h=h):
            at = pl.ds(pl.multiple_of(k * strip, strip), strip)
            wat = pl.ds(pl.multiple_of(h * wide + k * strip, strip), strip)
            part[:, at] = lax.dot_general(
                coeff, sw[wat, :], (((1,), (1,)), ((), ())), preferred_element_type=F32
            )
            return carry

        lax.fori_loop(0, wide // strip, grad_body, 0)
        for d in range(n):
            outbox[h, d] = part[pl.ds(d * row_dev, row_dev), :].astype(BF16)
        inbox[h, me] = outbox[h, me]

        def part_start(k, carry, h=h):
            part_copy(h, k).start()
            return carry

        lax.fori_loop(1, n, part_start, 0)

    for h in range(CUTS):

        def part_wait(k, carry, h=h):
            slot = lax.rem(me + k, n)
            pltpu.make_async_remote_copy(
                src_ref=inbox.at[h, slot],
                dst_ref=inbox.at[h, slot],
                send_sem=part_send.at[h, k],
                recv_sem=part_recv.at[h, slot],
                device_id={"blk": me},
                device_id_type=MESH,
            ).wait_recv()
            return carry

        lax.fori_loop(1, n, part_wait, 0)
        total = jnp.zeros((row_dev, wide), F32)
        for d in range(n):
            total = total + inbox[h, d].astype(F32)
        grad_ref[:, pl.ds(h * wide, wide)] = (total * omega).astype(BF16)

    for copy in sends:
        copy.wait_send()

    def drain(k, carry):
        stat_copy(k).wait_send()
        for h in range(CUTS):
            part_copy(h, k).wait_send()
        return carry

    lax.fori_loop(1, n, drain, 0)


def on_device(n, student_hidden, teacher_hidden, counts, student_head, teacher_head):
    row_dev, ds = student_hidden.shape
    dt = teacher_hidden.shape[2]
    vocab = student_head.shape[1]
    rows = n * row_dev
    padded = -(-rows // 128) * 128
    far = 4 if (n // 2) % 4 == 0 else 1
    wide = ds // CUTS
    loss, grad = pl.pallas_call(
        functools.partial(kernel, n, far),
        out_shape=(
            jax.ShapeDtypeStruct((row_dev, 128), F32),
            jax.ShapeDtypeStruct((row_dev, ds), BF16),
        ),
        in_specs=[
            pl.BlockSpec(memory_space=pltpu.SMEM),
            pl.BlockSpec(memory_space=pltpu.VMEM),
            pl.BlockSpec(memory_space=pltpu.VMEM),
            pl.BlockSpec(memory_space=pl.ANY),
            pl.BlockSpec(memory_space=pl.ANY),
        ],
        out_specs=(
            pl.BlockSpec(memory_space=pltpu.VMEM),
            pl.BlockSpec(memory_space=pltpu.VMEM),
        ),
        scratch_shapes=[
            pltpu.VMEM((n, row_dev, ds), BF16),
            pltpu.VMEM((n, row_dev, dt), BF16),
            pltpu.VMEM((rows, ds), F32),
            pltpu.VMEM((rows, dt), F32),
            pltpu.VMEM((ds, vocab), BF16),
            pltpu.VMEM((dt, vocab), BF16),
            pltpu.VMEM((rows, wide), F32),
            pltpu.VMEM((CUTS, n, row_dev, wide), BF16),
            pltpu.VMEM((CUTS, n, row_dev, wide), BF16),
            pltpu.VMEM((n, 8, padded), F32),
            pltpu.VMEM((padded, 128), F32),
            pltpu.SemaphoreType.DMA((2, 4)),
            pltpu.SemaphoreType.DMA((2, n)),
            pltpu.SemaphoreType.DMA((2, n)),
            pltpu.SemaphoreType.DMA((n,)),
            pltpu.SemaphoreType.DMA((n,)),
            pltpu.SemaphoreType.DMA((CUTS, n)),
            pltpu.SemaphoreType.DMA((CUTS, n)),
        ],
        compiler_params=pltpu.CompilerParams(
            collective_id=0, has_side_effects=True, vmem_limit_bytes=56 * 1024 * 1024
        ),
    )(counts, student_hidden, teacher_hidden.reshape(row_dev, dt), student_head, teacher_head.reshape(dt, vocab))
    return loss[:, 0], grad


def solution(mesh):
    return jax.shard_map(
        functools.partial(on_device, mesh.shape["blk"]),
        mesh=mesh,
        in_specs=(
            P(("group", "blk"), None),
            P(("group", "blk"), None, None),
            P(("group", "blk")),
            P("group", "blk"),
            P(None, "group", "blk"),
        ),
        out_specs=(P(("group", "blk")), P(("group", "blk"), None)),
        check_vma=False,
    )
```

time: 221 us -> 40.7 us (0.18)
  blocking collectives: 105 us -> 0 us
  waiting for transfers between devices: 84.9 us -> 0 us
  Pallas kernels: 0 us -> 37.2 us
  between operations: 15.4 us -> 0.64 us
  matrix products: 10.2 us -> 0 us
  other arithmetic: 4.36 us -> 0 us
    unnamed x2 -> x0, waiting for transfers between devices: 84.9 us -> none
    all_gather x2 -> x0, blocking collectives: 43.5 us -> none  [on_device(): lax.all_gather((student_hidden, teacher_hidden), 'blk', axis=0, tiled=True)]
    pallas_call x0 -> x1, Pallas kernels: none -> 37.2 us  [on_device(): pl.pallas_call(functools.partial(kernel, n, far), out_shape=(jax.ShapeDty...]
    pmax x1 -> x0, blocking collectives: 31.1 us -> none  [on_device(): lax.pmax((jnp.max(student_logit, axis=1), jnp.max(poe_score, axis=1)), 'b...]
    psum x1 -> x0, blocking collectives: 30 us -> none  [on_device(): lax.psum((jnp.sum(jnp.exp(student_logit - peak_student[:, None]), axis=1)...]
    dot_general x3 -> x0, matrix products: 10.2 us -> none  [the longest x1 4.98 us: on_device(): lax.dot_general(coeff, student_head, (((1,), (1,)), ((), ())), preferred_...]
  transfers between devices with their start and end apart: 1 -> 0, of which waited for: 1 -> 0; matrix products, arithmetic and copies ran while one was open for 1% -> 0% of each run, Pallas kernels for 0% -> 0%
where the time goes in v1:
time: 40.7 us; the launch traced here: 40.5 us
  Pallas kernels  37.2 us (91%)
  local copies, waits for them, and re-layouts  2.62 us (6%)
  between operations  0.64 us (2%)
    pallas_call x1, Pallas kernels, on_device(): pl.pallas_call(functools.partial(kernel, n, far), out_shape=(jax.ShapeDty...  37.2 us
    unnamed x1, local copies, waits for them, and re-layouts  1.33 us
    slice x1, local copies, waits for them, and re-layouts, on_device(): return (loss[:, 0], grad)  1.29 us

profile of v1, /device:TPU:0, one launch (start us, length us, event | category | flops | bytes accessed | tf_op | source)
XLA Modules:
  0.0 40.5 jit_solution(4122826865341879092)
XLA Ops:
  0.6 37.2 %shard_map.68 = (f32[2,128]{1,0:T(2,128)}, bf16[2,4096]{1,0:T(2,128)(2,1)}) custom-call(s32[2]{0:T(128)} %counts_ref.1, bf16[2,4096]{1,0:T(2,128)(2,1)} %sh_ref.1, bf16[2,5120]{1,0:T(2,128)(2,1)} %bitcast.3, bf16[4096,640]{1,0:T(8,128)(2,1)} %sw_ref.1, bf16[5120,640]{1,0:T(8,128)(2,1)} %bitcast.2), custom_call_target="tpu_custom_call" | custom-call | tf_op jit(solution)/shard_map/pallas_call | solution.py:280
  37.8 1.3 %slice_reduce_fusion = f32[2]{0:T(128)} fusion(f32[2,128]{1,0:T(2,128)} %get-tuple-element.4), kind=kLoop, calls=%fused_computation | loop fusion | bytes 16 | tf_op jit(solution)/shard_map/slice | solution.py:321
  39.1 1.3 %copy.8 = bf16[2,4096]{1,0:T(2,128)(2,1)} copy(bf16[2,4096]{1,0:T(2,128)(2,1)} %get-tuple-element.9) | data formatting | bytes 32768

commit v2 on v1

v2 whole, which is shorter than its diff:
```python
import functools

import jax
import jax.numpy as jnp
from jax import lax
from jax.experimental import pallas as pl
from jax.experimental.pallas import tpu as pltpu
from jax.sharding import PartitionSpec as P

MESH = pl.DeviceIdType.MESH
F32 = jnp.float32
BF16 = jnp.bfloat16
CUTS = 2
STEPS = 8


def kernel(
    n, counts_ref, sh_ref, th_ref, sw_ref, tw_ref, loss_ref, grad_ref,
    sheld, theld, xs, xt, sw, tw, part, core_in, outbox, inbox, stats, table,
    w_sem, send_sem, recv_sem, pair_send, pair_recv, stat_send, stat_recv,
    core_send, core_recv, part_send, part_recv,
):
    row_dev, ds = sh_ref.shape
    dt = th_ref.shape[1]
    rows = n * row_dev
    half = rows // 2
    chips = n // 2
    me = lax.axis_index("blk")
    core = lax.rem(me, 2)
    chip = me // 2
    other = me + 1 - 2 * core
    wide = ds // CUTS

    weights = []
    for which, (src, dst) in enumerate(((sw_ref, sw), (tw_ref, tw))):
        copy = pltpu.make_async_copy(src, dst, w_sem.at[which])
        copy.start()
        weights.append(copy)

    barrier = pltpu.get_barrier_semaphore()

    def greet(k, carry):
        pl.semaphore_signal(
            barrier, inc=1, device_id={"blk": lax.rem(me + k, n)}, device_id_type=MESH
        )
        return carry

    lax.fori_loop(1, n, greet, 0)
    pl.semaphore_wait(barrier, n - 1)

    owns = (sh_ref, th_ref)
    helds = (sheld, theld)

    def own_copy(which, k):
        return pltpu.make_async_remote_copy(
            src_ref=owns[which],
            dst_ref=helds[which].at[core, chip],
            send_sem=send_sem.at[which, k],
            recv_sem=recv_sem.at[which, chip],
            device_id={"blk": lax.rem(chip + k, chips) * 2 + core},
            device_id_type=MESH,
        )

    def pair_copy(which, k):
        slot = lax.rem(chip - k + chips, chips)
        return pltpu.make_async_remote_copy(
            src_ref=owns[which] if isinstance(k, int) and k == 0 else helds[which].at[core, slot],
            dst_ref=helds[which].at[core, slot],
            send_sem=pair_send.at[which, slot],
            recv_sem=pair_recv.at[which, slot],
            device_id={"blk": other},
            device_id_type=MESH,
        )

    def landed(which, k):
        slot = lax.rem(chip - k + chips, chips)
        pltpu.make_async_remote_copy(
            src_ref=helds[which].at[core, slot],
            dst_ref=helds[which].at[core, slot],
            send_sem=send_sem.at[which, 0],
            recv_sem=recv_sem.at[which, slot],
            device_id={"blk": other},
            device_id_type=MESH,
        ).wait_recv()

    def pair_landed(which, k):
        slot = lax.rem(chip - k + chips, chips)
        pltpu.make_async_remote_copy(
            src_ref=helds[which].at[1 - core, slot],
            dst_ref=helds[which].at[1 - core, slot],
            send_sem=send_sem.at[which, 0],
            recv_sem=pair_recv.at[which, slot],
            device_id={"blk": other},
            device_id_type=MESH,
        ).wait_recv()

    def loop(low, high, body):
        if high - low <= 16:
            for k in range(low, high):
                body(k)
        else:
            lax.fori_loop(low, high, lambda k, carry: (body(k), carry)[1], 0)

    for which in range(2):
        loop(1, chips, lambda k, which=which: own_copy(which, k).start())
        pair_copy(which, 0).start()

    def pass_on(which, k):
        landed(which, k)
        pair_copy(which, k).start()

    def settle(which, x):
        loop(0, chips, lambda k: pair_landed(which, k))
        for c in range(2):
            for d in range(chips):
                x[pl.ds(c * half + d * row_dev, row_dev), :] = helds[which][c, d].astype(F32)

    def term(x, w, k, total):
        cut = w.shape[0] // STEPS
        at = pl.ds(k * cut, cut)
        return total + jnp.dot(x[:, at].astype(BF16), w[at, :], preferred_element_type=F32)

    sheld[core, chip] = sh_ref[...]
    theld[core, chip] = th_ref[...]
    loop(1, chips, lambda k: pass_on(0, k))
    settle(0, xs)
    weights[0].wait()
    student = jnp.zeros((rows, sw.shape[1]), F32)
    share = -(-(chips - 1) // STEPS)
    for k in range(STEPS):
        student = term(xs, sw, k, student)
        loop(
            1 + k * share, max(1 + k * share, min(chips, 1 + (k + 1) * share)),
            lambda j: pass_on(1, j),
        )
    peak_s = jnp.max(student, axis=1, keepdims=True)
    exp_s = jnp.exp(student - peak_s)
    sum_s = jnp.sum(exp_s, axis=1, keepdims=True)
    settle(1, xt)
    weights[1].wait()
    score = jnp.zeros((rows, tw.shape[1]), F32)
    for k in range(STEPS):
        score = term(xt, tw, k, score)

    peak_p = jnp.max(score, axis=1, keepdims=True)
    exp_p = jnp.exp(score - peak_p)
    sum_p = jnp.sum(exp_p, axis=1, keepdims=True)
    weighted = jnp.sum(exp_p * (score - student), axis=1, keepdims=True)
    own_count = counts_ref[0]
    for r in range(1, row_dev):
        own_count = own_count + counts_ref[r]
    padded = table.shape[0]
    lane = lax.broadcasted_iota(jnp.int32, (rows, 128), 1)
    packed = jnp.where(lane == 5, own_count.astype(F32), 0.0)
    for k, column in enumerate((peak_s, sum_s, peak_p, sum_p, weighted)):
        packed = jnp.where(lane == k, column, packed)
    table[pl.ds(0, rows), :] = packed
    if padded > rows:
        table[pl.ds(rows, padded - rows), :] = jnp.zeros((padded - rows, 128), F32)
    stats[me] = jnp.transpose(table[...])[:8, :]

    def stat_copy(k):
        return pltpu.make_async_remote_copy(
            src_ref=stats.at[me],
            dst_ref=stats.at[me],
            send_sem=stat_send.at[k],
            recv_sem=stat_recv.at[me],
            device_id={"blk": lax.rem(me + k, n)},
            device_id_type=MESH,
        )

    def stat_landed(k):
        slot = lax.rem(me + k, n)
        pltpu.make_async_remote_copy(
            src_ref=stats.at[slot],
            dst_ref=stats.at[slot],
            send_sem=stat_send.at[k],
            recv_sem=stat_recv.at[slot],
            device_id={"blk": other},
            device_id_type=MESH,
        ).wait_recv()

    loop(1, n, lambda k: stat_copy(k).start())

    high_s = exp_s.astype(BF16)
    high_p = exp_p.astype(BF16)
    low_s = (exp_s - high_s.astype(F32)).astype(BF16)
    low_p = (exp_p - high_p.astype(F32)).astype(BF16)
    stacked = jnp.concatenate([high_s, low_s, high_p, low_p], axis=0)
    strip = 512 if wide % 512 == 0 else wide

    def raw(h, k):
        return lax.dot_general(
            stacked, sw[pl.ds(h * wide + k * strip, strip), :], (((1,), (1,)), ((), ())),
            preferred_element_type=F32,
        )

    def scaled(value, scale_s, scale_p):
        return scale_s * (value[:rows] + value[rows:2 * rows]) - scale_p * (
            value[2 * rows:3 * rows] + value[3 * rows:]
        )

    early = [raw(0, k) for k in range(wide // strip)]
    loop(1, n, stat_landed)

    all_stats = stats[...]
    top_s = jnp.max(all_stats[:, 0:1, :], axis=0)
    top_p = jnp.max(all_stats[:, 2:3, :], axis=0)
    change_p = jnp.exp(all_stats[:, 2:3, :] - top_p[None])
    total_s = jnp.sum(jnp.exp(all_stats[:, 0:1, :] - top_s[None]) * all_stats[:, 1:2, :], axis=0)
    total_p = jnp.sum(change_p * all_stats[:, 3:4, :], axis=0)
    total_w = jnp.sum(change_p * all_stats[:, 4:5, :], axis=0)
    total_count = jnp.sum(all_stats[:, 5:6, :], axis=0)
    lse_s = top_s + jnp.log(total_s)
    lse_p = top_p + jnp.log(total_p)
    divergence = total_w / total_p - lse_p + lse_s
    line = lax.broadcasted_iota(jnp.int32, (128, padded), 0)
    merged = jnp.where(line == 0, lse_s, 0.0)
    merged = jnp.where(line == 1, lse_p, merged)
    merged = jnp.where(line == 2, divergence, merged)
    merged = jnp.where(line == 3, total_count, merged)
    table[...] = jnp.transpose(merged)
    scale_s = jnp.exp(peak_s - table[pl.ds(0, rows), 0:1])
    scale_p = jnp.exp(peak_p - table[pl.ds(0, rows), 1:2])

    own_rows = table[pl.ds(core * half + chip * row_dev, row_dev), :]
    row = lax.broadcasted_iota(jnp.int32, (row_dev, 1), 0)
    own_counts = jnp.zeros((row_dev, 1), F32)
    for r in range(row_dev):
        own_counts = jnp.where(row == r, counts_ref[r].astype(F32), own_counts)
    omega = own_counts * rows / own_rows[:, 3:4]
    loss_ref[...] = jnp.broadcast_to(omega * own_rows[:, 2:3], loss_ref.shape)

    def core_copy(h):
        return pltpu.make_async_remote_copy(
            src_ref=part.at[h, pl.ds(pl.multiple_of((1 - core) * half, 8), half)],
            dst_ref=core_in.at[h],
            send_sem=core_send.at[h],
            recv_sem=core_recv.at[h],
            device_id={"blk": other},
            device_id_type=MESH,
        )

    def part_copy(h, k):
        target = lax.rem(chip + k, chips)
        return pltpu.make_async_remote_copy(
            src_ref=outbox.at[h, target],
            dst_ref=inbox.at[h, chip],
            send_sem=part_send.at[h, k],
            recv_sem=part_recv.at[h, chip],
            device_id={"blk": target * 2 + core},
            device_id_type=MESH,
        )

    def part_landed(h, k):
        slot = lax.rem(chip + k, chips)
        pltpu.make_async_remote_copy(
            src_ref=inbox.at[h, slot],
            dst_ref=inbox.at[h, slot],
            send_sem=part_send.at[h, k],
            recv_sem=part_recv.at[h, slot],
            device_id={"blk": other},
            device_id_type=MESH,
        ).wait_recv()

    def hand_on(h):
        core_copy(h).wait_recv()
        core_in[h] = core_in[h] + part[h, pl.ds(pl.multiple_of(core * half, 8), half), :]
        for d in range(chips):
            outbox[h, d] = core_in[h, pl.ds(d * row_dev, row_dev), :].astype(BF16)
        inbox[h, chip] = outbox[h, chip]
        loop(1, chips, lambda k: part_copy(h, k).start())

    for h in range(CUTS):
        for k in range(wide // strip):
            value = early[k] if h == 0 else raw(h, k)
            part[h, :, pl.ds(k * strip, strip)] = scaled(value, scale_s, scale_p)
        core_copy(h).start()
        if h:
            hand_on(h - 1)
    hand_on(CUTS - 1)

    for h in range(CUTS):
        loop(1, chips, lambda k: part_landed(h, k))
        total = jnp.zeros((row_dev, wide), F32)
        for d in range(chips):
            total = total + inbox[h, d].astype(F32)
        grad_ref[:, pl.ds(h * wide, wide)] = (total * omega).astype(BF16)

    def drain(k):
        for which in range(2):
            own_copy(which, k).wait_send()
            pair_copy(which, k).wait_send()
        for h in range(CUTS):
            part_copy(h, k).wait_send()

    loop(1, chips, drain)
    for which in range(2):
        pair_copy(which, 0).wait_send()
    for h in range(CUTS):
        core_copy(h).wait_send()
    loop(1, n, lambda k: stat_copy(k).wait_send())


def finish(loss_in, grad_in, loss_ref, grad_ref):
    for r in range(loss_ref.shape[0]):
        loss_ref[r] = loss_in[r, 0]
    grad_ref[...] = grad_in[...]


def on_device(n, student_hidden, teacher_hidden, counts, student_head, teacher_head):
    row_dev, ds = student_hidden.shape
    dt = teacher_hidden.shape[2]
    vocab = student_head.shape[1]
    rows = n * row_dev
    half = rows // 2
    chips = n // 2
    padded = -(-rows // 128) * 128
    wide = ds // CUTS
    dma = pltpu.SemaphoreType.DMA
    loss, grad = pl.pallas_call(
        functools.partial(kernel, n),
        out_shape=(
            jax.ShapeDtypeStruct((row_dev, 128), F32),
            jax.ShapeDtypeStruct((row_dev, ds), BF16),
        ),
        in_specs=[
            pl.BlockSpec(memory_space=pltpu.SMEM),
            pl.BlockSpec(memory_space=pltpu.VMEM),
            pl.BlockSpec(memory_space=pltpu.VMEM),
            pl.BlockSpec(memory_space=pl.ANY),
            pl.BlockSpec(memory_space=pl.ANY),
        ],
        out_specs=(
            pl.BlockSpec(memory_space=pltpu.VMEM),
            pl.BlockSpec(memory_space=pltpu.VMEM),
        ),
        scratch_shapes=[
            pltpu.VMEM((2, chips, row_dev, ds), BF16),
            pltpu.VMEM((2, chips, row_dev, dt), BF16),
            pltpu.VMEM((rows, ds), F32),
            pltpu.VMEM((rows, dt), F32),
            pltpu.VMEM((ds, vocab), BF16),
            pltpu.VMEM((dt, vocab), BF16),
            pltpu.VMEM((CUTS, rows, wide), F32),
            pltpu.VMEM((CUTS, half, wide), F32),
            pltpu.VMEM((CUTS, chips, row_dev, wide), BF16),
            pltpu.VMEM((CUTS, chips, row_dev, wide), BF16),
            pltpu.VMEM((n, 8, padded), F32),
            pltpu.VMEM((padded, 128), F32),
            dma((2,)),
            dma((2, chips)),
            dma((2, chips)),
            dma((2, chips)),
            dma((2, chips)),
            dma((n,)),
            dma((n,)),
            dma((CUTS,)),
            dma((CUTS,)),
            dma((CUTS, chips)),
            dma((CUTS, chips)),
        ],
        compiler_params=pltpu.CompilerParams(
            collective_id=0, has_side_effects=True, vmem_limit_bytes=56 * 1024 * 1024
        ),
    )(counts, student_hidden, teacher_hidden.reshape(row_dev, dt), student_head, teacher_head.reshape(dt, vocab))
    loss, grad = pl.pallas_call(
        finish,
        out_shape=(
            jax.ShapeDtypeStruct((row_dev,), F32),
            jax.ShapeDtypeStruct((row_dev, ds), BF16),
        ),
        in_specs=[
            pl.BlockSpec(memory_space=pltpu.SMEM),
            pl.BlockSpec(memory_space=pltpu.VMEM),
        ],
        out_specs=(
            pl.BlockSpec(memory_space=pltpu.SMEM),
            pl.BlockSpec(memory_space=pltpu.VMEM),
        ),
    )(loss, grad)
    return loss, grad


def solution(mesh):
    return jax.shard_map(
        functools.partial(on_device, mesh.shape["blk"]),
        mesh=mesh,
        in_specs=(
            P(("group", "blk"), None),
            P(("group", "blk"), None, None),
            P(("group", "blk")),
            P("group", "blk"),
            P(None, "group", "blk"),
        ),
        out_specs=(P(("group", "blk")), P(("group", "blk"), None)),
        check_vma=False,
    )
```

time: 40.7 us -> 32.7 us (0.80)
  Pallas kernels: 37.2 us -> 31.9 us
  local copies, waits for them, and re-layouts: 2.62 us -> 0 us
    pallas_call x1 -> x2, Pallas kernels: 37.2 us -> 31.9 us  [the longest x1 30.5 us: on_device(): pl.pallas_call(functools.partial(kernel, n), out_shape=(jax.ShapeDtypeStr...]
    unnamed x1 -> x0, local copies, waits for them, and re-layouts: 1.33 us -> none
    slice x1 -> x0, local copies, waits for them, and re-layouts: 1.29 us -> none  [on_device(): return (loss[:, 0], grad)]
where the time goes in v2:
time: 32.7 us; the launch traced here: 32.5 us
  Pallas kernels  31.9 us (98%)
  between operations  0.64 us (2%)
    pallas_call x1, Pallas kernels, on_device(): pl.pallas_call(functools.partial(kernel, n), out_shape=(jax.ShapeDtypeStr...  30.5 us
    pallas_call x1, Pallas kernels, on_device(): pl.pallas_call(finish, out_shape=(jax.ShapeDtypeStruct((row_dev,), F32),...  1.34 us

profile of v2, /device:TPU:0, one launch (start us, length us, event | category | flops | bytes accessed | tf_op | source)
XLA Modules:
  0.0 32.5 jit_solution(2543114692544775200)
XLA Ops:
  0.6 30.5 %shard_map.68 = (f32[2,128]{1,0:T(2,128)}, bf16[2,4096]{1,0:T(2,128)(2,1)}) custom-call(s32[2]{0:T(128)} %counts_ref.1, bf16[2,4096]{1,0:T(2,128)(2,1)} %sh_ref.1, bf16[2,5120]{1,0:T(2,128)(2,1)} %bitcast.3, bf16[4096,640]{1,0:T(8,128)(2,1)} %sw_ref.1, bf16[5120,640]{1,0:T(8,128)(2,1)} %bitcast.2), custom_call_target="tpu_custom_call" | custom-call | tf_op jit(solution)/shard_map/pallas_call | solution.py:321
  31.2 1.3 %shard_map.69 = (f32[2]{0:T(128)}, bf16[2,4096]{1,0:T(2,128)(2,1)}) custom-call(f32[2,128]{1,0:T(2,128)} %get-tuple-element.4.loss_in, bf16[2,4096]{1,0:T(2,128)(2,1)} %get-tuple-element.5.grad_in), custom_call_target="tpu_custom_call" | custom-call | tf_op jit(solution)/shard_map/pallas_call | solution.py:367

commit v3 on v2

--- a/solution.py
+++ b/solution.py
@@ -10,8 +10,8 @@
 MESH = pl.DeviceIdType.MESH
 F32 = jnp.float32
 BF16 = jnp.bfloat16
-CUTS = 2
-STEPS = 8
+CUTS = 1
+STEPS = 4
 
 
 def kernel(
@@ -195,12 +195,25 @@
             preferred_element_type=F32,
         )
 
-    def scaled(value, scale_s, scale_p):
-        return scale_s * (value[:rows] + value[rows:2 * rows]) - scale_p * (
-            value[2 * rows:3 * rows] + value[3 * rows:]
-        )
-
-    early = [raw(0, k) for k in range(wide // strip)]
+    def core_copy(h):
+        return pltpu.make_async_remote_copy(
+            src_ref=part.at[h, :, pl.ds(pl.multiple_of((1 - core) * half, 8), half)],
+            dst_ref=core_in.at[h],
+            send_sem=core_send.at[h],
+            recv_sem=core_recv.at[h],
+            device_id={"blk": other},
+            device_id_type=MESH,
+        )
+
+    for h in range(CUTS):
+        for k in range(wide // strip):
+            value = raw(h, k)
+            for m in range(2):
+                part[h, m, :, pl.ds(k * strip, strip)] = (
+                    value[2 * m * rows:(2 * m + 1) * rows]
+                    + value[(2 * m + 1) * rows:(2 * m + 2) * rows]
+                )
+        core_copy(h).start()
     loop(1, n, stat_landed)
 
     all_stats = stats[...]
@@ -219,9 +232,12 @@
     merged = jnp.where(line == 1, lse_p, merged)
     merged = jnp.where(line == 2, divergence, merged)
     merged = jnp.where(line == 3, total_count, merged)
+    for k, device in enumerate((me, other)):
+        merged = jnp.where(line == 4 + 2 * k, jnp.exp(stats[device, 0:1, :] - lse_s), merged)
+        merged = jnp.where(line == 5 + 2 * k, jnp.exp(stats[device, 2:3, :] - lse_p), merged)
     table[...] = jnp.transpose(merged)
-    scale_s = jnp.exp(peak_s - table[pl.ds(0, rows), 0:1])
-    scale_p = jnp.exp(peak_p - table[pl.ds(0, rows), 1:2])
+    kept = pl.ds(pl.multiple_of(core * half, 8), half)
+    scales = table[kept, :]
 
     own_rows = table[pl.ds(core * half + chip * row_dev, row_dev), :]
     row = lax.broadcasted_iota(jnp.int32, (row_dev, 1), 0)
@@ -231,16 +247,6 @@
     omega = own_counts * rows / own_rows[:, 3:4]
     loss_ref[...] = jnp.broadcast_to(omega * own_rows[:, 2:3], loss_ref.shape)
 
-    def core_copy(h):
-        return pltpu.make_async_remote_copy(
-            src_ref=part.at[h, pl.ds(pl.multiple_of((1 - core) * half, 8), half)],
-            dst_ref=core_in.at[h],
-            send_sem=core_send.at[h],
-            recv_sem=core_recv.at[h],
-            device_id={"blk": other},
-            device_id_type=MESH,
-        )
-
     def part_copy(h, k):
         target = lax.rem(chip + k, chips)
         return pltpu.make_async_remote_copy(
@@ -263,22 +269,16 @@
             device_id_type=MESH,
         ).wait_recv()
 
-    def hand_on(h):
+    for h in range(CUTS):
         core_copy(h).wait_recv()
-        core_in[h] = core_in[h] + part[h, pl.ds(pl.multiple_of(core * half, 8), half), :]
+        total = scales[:, 4:5] * part[h, 0, kept, :] - scales[:, 5:6] * part[h, 1, kept, :]
+        core_in[h, 0] = total + (
+            scales[:, 6:7] * core_in[h, 0] - scales[:, 7:8] * core_in[h, 1]
+        )
         for d in range(chips):
-            outbox[h, d] = core_in[h, pl.ds(d * row_dev, row_dev), :].astype(BF16)
+            outbox[h, d] = core_in[h, 0, pl.ds(d * row_dev, row_dev), :].astype(BF16)
         inbox[h, chip] = outbox[h, chip]
         loop(1, chips, lambda k: part_copy(h, k).start())
-
-    for h in range(CUTS):
-        for k in range(wide // strip):
-            value = early[k] if h == 0 else raw(h, k)
-            part[h, :, pl.ds(k * strip, strip)] = scaled(value, scale_s, scale_p)
-        core_copy(h).start()
-        if h:
-            hand_on(h - 1)
-    hand_on(CUTS - 1)
 
     for h in range(CUTS):
         loop(1, chips, lambda k: part_landed(h, k))
@@ -342,8 +342,8 @@
             pltpu.VMEM((rows, dt), F32),
             pltpu.VMEM((ds, vocab), BF16),
             pltpu.VMEM((dt, vocab), BF16),
-            pltpu.VMEM((CUTS, rows, wide), F32),
-            pltpu.VMEM((CUTS, half, wide), F32),
+            pltpu.VMEM((CUTS, 2, rows, wide), F32),
+            pltpu.VMEM((CUTS, 2, half, wide), F32),
             pltpu.VMEM((CUTS, chips, row_dev, wide), BF16),
             pltpu.VMEM((CUTS, chips, row_dev, wide), BF16),
             pltpu.VMEM((n, 8, padded), F32),

time: 32.7 us -> 30.7 us (0.939)
  Pallas kernels: 31.9 us -> 29.8 us
    pallas_call x1, Pallas kernels: 30.5 us -> 28.5 us  [on_device(): pl.pallas_call(functools.partial(kernel, n), out_shape=(jax.ShapeDtypeStr...]
where the time goes in v3:
time: 30.7 us; the launch traced here: 30.5 us
  Pallas kernels  29.8 us (97%)
  between operations  0.64 us (2%)
    pallas_call x1, Pallas kernels, on_device(): pl.pallas_call(functools.partial(kernel, n), out_shape=(jax.ShapeDtypeStr...  28.5 us
    pallas_call x1, Pallas kernels, on_device(): pl.pallas_call(finish, out_shape=(jax.ShapeDtypeStruct((row_dev,), F32),...  1.34 us

profile of v3, /device:TPU:0, one launch (start us, length us, event | category | flops | bytes accessed | tf_op | source)
XLA Modules:
  0.0 30.5 jit_solution(5761378850552129001)
XLA Ops:
  0.6 28.5 %shard_map.68 = (f32[2,128]{1,0:T(2,128)}, bf16[2,4096]{1,0:T(2,128)(2,1)}) custom-call(s32[2]{0:T(128)} %counts_ref.1, bf16[2,4096]{1,0:T(2,128)(2,1)} %sh_ref.1, bf16[2,5120]{1,0:T(2,128)(2,1)} %bitcast.3, bf16[4096,640]{1,0:T(8,128)(2,1)} %sw_ref.1, bf16[5120,640]{1,0:T(8,128)(2,1)} %bitcast.2), custom_call_target="tpu_custom_call" | custom-call | tf_op jit(solution)/shard_map/pallas_call | solution.py:321
  29.1 1.3 %shard_map.69 = (f32[2]{0:T(128)}, bf16[2,4096]{1,0:T(2,128)(2,1)}) custom-call(f32[2,128]{1,0:T(2,128)} %get-tuple-element.4.loss_in, bf16[2,4096]{1,0:T(2,128)(2,1)} %get-tuple-element.5.grad_in), custom_call_target="tpu_custom_call" | custom-call | tf_op jit(solution)/shard_map/pallas_call | solution.py:367

commit v4 on v3

--- a/solution.py
+++ b/solution.py
@@ -252,7 +252,7 @@
         return pltpu.make_async_remote_copy(
             src_ref=outbox.at[h, target],
             dst_ref=inbox.at[h, chip],
-            send_sem=part_send.at[h, k],
+            send_sem=part_send.at[h, target],
             recv_sem=part_recv.at[h, chip],
             device_id={"blk": target * 2 + core},
             device_id_type=MESH,
@@ -277,8 +277,12 @@
         )
         for d in range(chips):
             outbox[h, d] = core_in[h, 0, pl.ds(d * row_dev, row_dev), :].astype(BF16)
+
+            @pl.when(chip != d)
+            def _():
+                part_copy(h, d - chip + chips).start()
+
         inbox[h, chip] = outbox[h, chip]
-        loop(1, chips, lambda k: part_copy(h, k).start())
 
     for h in range(CUTS):
         loop(1, chips, lambda k: part_landed(h, k))

time: 30.7 us -> 30.6 us (level)
  no operation moved by 1% of the time
where the time goes in v4:
time: 30.6 us; the launch traced here: 30.4 us
  Pallas kernels  29.8 us (97%)
  between operations  0.64 us (2%)
    pallas_call x1, Pallas kernels, on_device(): pl.pallas_call(functools.partial(kernel, n), out_shape=(jax.ShapeDtypeStr...  28.4 us
    pallas_call x1, Pallas kernels, on_device(): pl.pallas_call(finish, out_shape=(jax.ShapeDtypeStruct((row_dev,), F32),...  1.34 us

profile of v4, /device:TPU:0, one launch (start us, length us, event | category | flops | bytes accessed | tf_op | source)
XLA Modules:
  0.0 30.4 jit_solution(18349345073305023301)
XLA Ops:
  0.6 28.4 %shard_map.68 = (f32[2,128]{1,0:T(2,128)}, bf16[2,4096]{1,0:T(2,128)(2,1)}) custom-call(s32[2]{0:T(128)} %counts_ref.1, bf16[2,4096]{1,0:T(2,128)(2,1)} %sh_ref.1, bf16[2,5120]{1,0:T(2,128)(2,1)} %bitcast.3, bf16[4096,640]{1,0:T(8,128)(2,1)} %sw_ref.1, bf16[5120,640]{1,0:T(8,128)(2,1)} %bitcast.2), custom_call_target="tpu_custom_call" | custom-call | tf_op jit(solution)/shard_map/pallas_call | solution.py:325
  29.1 1.3 %shard_map.69 = (f32[2]{0:T(128)}, bf16[2,4096]{1,0:T(2,128)(2,1)}) custom-call(f32[2,128]{1,0:T(2,128)} %get-tuple-element.4.loss_in, bf16[2,4096]{1,0:T(2,128)(2,1)} %get-tuple-element.5.grad_in), custom_call_target="tpu_custom_call" | custom-call | tf_op jit(solution)/shard_map/pallas_call | solution.py:371
